TPU v7x, 128 devices: a whole 4x4x4 slice. The times are simulated.
128 devices in a mesh: grp: 2 (over core), ty: 8 (over x_lo, y), tx: 8 (over x_hi, z).
Axes of the slice: x: 4 (x_hi: 2, x_lo: 2; x = x_hi * 2 + x_lo), y: 4, z: 4, core: 2. Of those that a mesh axis runs over, the one named last changes fastest.
Arguments:
- coupled_state: float32 [2, 23, 32, 16, 1024], P('grp', None, None, 'ty', 'tx'), may hold values from -4 to 4, as said below
- land_mask: int32 [16, 1024], P('ty', 'tx'), may hold values 0 or 1
- bottom_level: int32 [16, 1024], P('ty', 'tx'), may hold values from 1 to 32
- shortwave: float32 [16, 1024], P('ty', 'tx'), may hold values from 0.5 to 1.5
- absorb: float32 [19], replicated, may hold values from 0.01 to 0.1
- reaction: float32 [19, 19], replicated, may hold values from -1.25 to 1.25
Outputs:
- new_state: float32 [2, 23, 32, 16, 1024], P('grp', None, None, 'ty', 'tx')
Inputs may be any that keep to these rules, and one draw needn't show every extreme that they name: `coupled_state`: fields 0 and 1 lie in -2 to 2, fields 2 and 3 in -4 to 4, the tracers in 0.1 to 2.
All inputs are finite; a program needn't handle non-finite values. No bound on the sum of `land_mask` on one device may be relied on, other than what follows from the above.
Results may differ from a plain program's by a relative error of at most 0.0003.
Values sent between devices are 32-bit elements; how exact they have to be, the bound alone decides.
A program may use at most 192 MiB of HBM per device.

v0:
```python
import functools

import jax
import jax.numpy as jnp
from jax import lax
from jax.experimental import pallas as pl
from jax.experimental.pallas import tpu as pltpu
from jax.sharding import PartitionSpec as P

STEPS = 2
NF = 23
NT = 19
NZ = 32
CH = 8
NK = NZ // CH
MESH = pl.DeviceIdType.MESH
F32 = jnp.float32

integration_interval = 0.1
tracer_step = 0.08
coriolis = 0.8
barotropic_gradient_coefficient = 0.1
water_extinction = 0.04
layer_depth = 0.05
growth_peak = 2.0
half_light = 0.5
ratio_floor = 0.01

DIAGS = ((-1, -1), (-1, 1), (1, -1), (1, 1))


def lanes(shape):
    return lax.broadcasted_iota(jnp.int32, shape, len(shape) - 1)


def roll(x, shift):
    return pltpu.roll(x, shift % 128 if isinstance(shift, int) else shift, x.ndim - 1)


def cumulative(x):
    n = x.shape[0]
    level = lax.broadcasted_iota(jnp.int32, x.shape, 0)
    d = 1
    while d < n:
        x = x + jnp.where(level >= d, pltpu.roll(x, d, 0), 0.0)
        d *= 2
    return x


def inverse(x):
    r = pl.reciprocal(x, approx=True)
    return r * (2.0 - x * r)


def kernel(
    x, land, bottom, shortwave, absorb, reaction, out,
    V, H, PS, PT, PD, ADV, CO, ZC, ZS, D, DH, SS, ST, KD,
    lsem, row_s, row_r, col_s, col_r, diag_s, diag_r, dyn_s, dyn_r, tra_s, tra_r, ors, orr, ocs, ocr,
):
    grp, ty, tx = lax.axis_index("grp"), lax.axis_index("ty"), lax.axis_index("tx")
    nty, ntx = lax.axis_size("ty"), lax.axis_size("tx")
    has_y = (ty > 0, ty < nty - 1)
    has_x = (tx > 0, tx < ntx - 1)
    step_of = (-1, 1)

    def has_diag(i):
        a, b = DIAGS[i]
        return has_y[(a + 1) // 2] & has_x[(b + 1) // 2]

    barrier = pltpu.get_barrier_semaphore()
    count = jnp.int32(1)
    pl.semaphore_signal(barrier, inc=1, device_id={"grp": 1 - grp}, device_id_type=MESH)
    for d in range(2):
        count = count + has_y[d].astype(jnp.int32) + has_x[d].astype(jnp.int32)

        @pl.when(has_y[d])
        def _():
            pl.semaphore_signal(barrier, inc=1, device_id={"ty": ty + step_of[d]}, device_id_type=MESH)

        @pl.when(has_x[d])
        def _():
            pl.semaphore_signal(barrier, inc=1, device_id={"tx": tx + step_of[d]}, device_id_type=MESH)

    load = pltpu.make_async_copy(x, V.at[0], lsem.at[0])
    load.start()

    def fill(ref, n):
        def body(i, c):
            ref[i] = jnp.zeros(ref.shape[1:], F32)
            return c

        lax.fori_loop(0, n, body, 0)

    lane8 = lanes((CH, 128))
    four8 = lane8 % 4
    first, last = lane8 == 0, lane8 == 127

    def tracer_side():
        n_diag = jnp.int32(0)
        for i in range(4):
            n_diag = n_diag + has_diag(i).astype(jnp.int32)

            @pl.when(has_diag(i))
            def _():
                a, b = DIAGS[i]
                pl.semaphore_signal(barrier, inc=1, device_id={"ty": ty + a, "tx": tx + b}, device_id_type=MESH)

            @pl.when(jnp.logical_not(has_diag(i)))
            def _():
                for s in range(STEPS):
                    PD[s, i] = jnp.zeros(PD.shape[2:], F32)

        for d in range(2):
            @pl.when(jnp.logical_not(has_y[d]))
            def _():
                for s in range(STEPS):
                    fill(H.at[s, d], NF)

            @pl.when(jnp.logical_not(has_x[d]))
            def _():
                for s in range(STEPS):
                    fill(PT.at[s, d], 2)

        def row_copy(s, d, k, part):
            lo, n = ((0, 2), (4, NT))[part]
            rows = pl.ds(pl.multiple_of(k * 16, 16), 16)
            src = (x if s == 0 else V.at[s]).at[pl.ds(lo, n), rows]
            return pltpu.make_async_remote_copy(
                src_ref=src,
                dst_ref=H.at[s, 1 - d, pl.ds(lo, n), rows],
                send_sem=row_s.at[s, d, k, part],
                recv_sem=row_r.at[s, 1 - d, k, part],
                device_id={"ty": ty + step_of[d]},
                device_id_type=MESH,
            )

        def row_arrival(s, d, k, part):
            lo, n = ((0, 2), (4, NT))[part]
            rows = pl.ds(pl.multiple_of(k * 16, 16), 16)
            return pltpu.make_async_remote_copy(
                src_ref=V.at[s, pl.ds(lo, n), rows],
                dst_ref=H.at[s, d, pl.ds(lo, n), rows],
                send_sem=row_s.at[s, d, k, part],
                recv_sem=row_r.at[s, d, k, part],
                device_id={"ty": ty + step_of[d]},
                device_id_type=MESH,
            )

        def col_copy(s, d, k, arrival=False):
            lev = pl.ds(pl.multiple_of(k * CH, CH), CH)
            to = d if arrival else 1 - d
            return pltpu.make_async_remote_copy(
                src_ref=PS.at[s, :, lev],
                dst_ref=PT.at[s, to, :, lev],
                send_sem=col_s.at[s, d, k],
                recv_sem=col_r.at[s, to, k],
                device_id={"tx": tx + step_of[d]},
                device_id_type=MESH,
            )

        def diag_copy(s, i, k, arrival=False):
            a, b = DIAGS[i]
            lev = pl.ds(pl.multiple_of(k * CH, CH), CH)
            to = i if arrival else 3 - i
            return pltpu.make_async_remote_copy(
                src_ref=PS.at[s, (a + 1) // 2, lev],
                dst_ref=PD.at[s, to, lev],
                send_sem=diag_s.at[s, i, k],
                recv_sem=diag_r.at[s, to, k],
                device_id={"ty": ty + a, "tx": tx + b},
                device_id_type=MESH,
            )

        def each_row(s, k, act):
            for d in range(2):
                @pl.when(has_y[d])
                def _():
                    for part in range(2):
                        act(s, d, k, part)

        def send_rows(s, k):
            each_row(s, k, lambda *a: row_copy(*a).start())

        def send_edges(s, k):
            for d in range(2):
                @pl.when(has_x[d])
                def _():
                    col_copy(s, d, k).start()
            for i in range(4):
                @pl.when(has_diag(i))
                def _():
                    diag_copy(s, i, k).start()

        def receive(s, k):
            for d in range(2):
                @pl.when(has_x[d])
                def _():
                    col_copy(s, d, k, True).wait_recv()
            for i in range(4):
                @pl.when(has_diag(i))
                def _():
                    diag_copy(s, i, k, True).wait_recv()
            each_row(s, k, lambda *a: row_arrival(*a).wait_recv())

        def sent(s, k):
            each_row(s, k, lambda *a: row_copy(*a).wait_send())
            for d in range(2):
                @pl.when(has_x[d])
                def _():
                    col_copy(s, d, k).wait_send()
            for i in range(4):
                @pl.when(has_diag(i))
                def _():
                    diag_copy(s, i, k).wait_send()

        def tracers_over(k):
            rows = pl.ds(pl.multiple_of(k * 16, 16), 16)
            return pltpu.make_async_remote_copy(
                src_ref=V.at[1, pl.ds(4, NT), rows],
                dst_ref=V.at[2, pl.ds(4, NT), rows],
                send_sem=tra_s.at[k],
                recv_sem=tra_r.at[k],
                device_id={"grp": 1 - grp},
                device_id_type=MESH,
            )

        def store_out(k):
            rows = pl.ds(pl.multiple_of(k * 16, 16), 16)
            return pltpu.make_async_copy(V.at[2, pl.ds(4, NT), rows], out.at[pl.ds(4, NT), rows], lsem.at[1 + k])

        def pack(s, start, count):
            lane = lanes((count, 128))
            quarter = lane // 4

            def body(f, rows):
                shift = 4 * f + 2
                return tuple(
                    jnp.where(quarter == f, roll(V[s, f, pl.ds(2 * start + r, count, 2), :], shift), rows[r])
                    for r in range(2)
                )

            zero = jnp.zeros((count, 128), F32)
            packed = lax.fori_loop(0, NF, body, (zero, zero))
            for r in range(2):
                PS[s, r, pl.ds(start, count), :] = packed[r]

        def chunk(s, k, carry):
            base = k * 16
            lev = pl.ds(pl.multiple_of(k * CH, CH), CH)

            def row(f, r):
                at = pl.ds(base + r % 2, CH, 2)
                if r < 0:
                    return H[s, 0, f, at, :]
                if r > 1:
                    return H[s, 1, f, at, :]
                return V[s, f, at, :]

            y_lo = jnp.where(has_y[0], 0.02, 0.0).astype(F32)
            y_hi = jnp.where(has_y[1], 0.02, 0.0).astype(F32)
            x_lo = jnp.where(has_x[0], 0.02, 0.0).astype(F32)
            x_hi = jnp.where(has_x[1], 0.02, 0.0).astype(F32)
            right = four8 == 1
            left = four8 == 2

            own = [PS[s, r, lev, :] for r in range(2)]
            low = [PD[s, 0, lev, :], PT[s, 0, 0, lev, :], PT[s, 0, 1, lev, :], PD[s, 2, lev, :]]
            high = [PD[s, 1, lev, :], PT[s, 1, 0, lev, :], PT[s, 1, 1, lev, :], PD[s, 3, lev, :]]
            mid = [jnp.where(right, roll(high[i], -1), roll(low[i], 1)) for i in range(4)]
            for i in range(4):
                ZC[i] = mid[i]
            north = [jnp.where(right, roll(high[1 + r], -2), own[r]) for r in range(2)]
            south = [jnp.where(right, own[r], roll(low[1 + r], 2)) for r in range(2)]

            def spread(value, f):
                value = jnp.where(lane8 // 4 == f, value, 0.0)
                for d in (4, 8, 16, 32, 64):
                    value = value + roll(value, d)
                return value

            def face(q, a, b):
                anti = jnp.abs(q) * (b - a)
                return anti, q * (a + b) - anti

            def bounds(centre, others):
                hi = lo = centre
                for o in others:
                    hi, lo = jnp.maximum(hi, o), jnp.minimum(lo, o)
                return hi, lo

            def gains(w, e, n, so):
                gain_in = (jnp.maximum(w, 0.0) - jnp.minimum(e, 0.0)) + (jnp.maximum(so, 0.0) - jnp.minimum(n, 0.0))
                gain_out = (jnp.maximum(e, 0.0) - jnp.minimum(w, 0.0)) + (jnp.maximum(n, 0.0) - jnp.minimum(so, 0.0))
                return gain_in, gain_out

            def ratio(gain, room):
                return jnp.minimum(gain, jnp.maximum(room, 0.0)) * inverse(
                    jnp.maximum(gain, ratio_floor * tracer_step)
                )

            u_mid = [spread(m, 0) for m in mid]
            q_rows = [
                (u_mid[0] + u_mid[1]) * y_lo,
                (u_mid[1] + u_mid[2]) * 0.02,
                (u_mid[2] + u_mid[3]) * y_hi,
            ]
            faces = [face(q_rows[i], mid[i], mid[i + 1]) for i in range(3)]
            for r in range(2):
                v_mid = spread(mid[1 + r], 1)
                q_n = (v_mid + spread(north[r], 1)) * jnp.where(left, x_lo, 0.02)
                q_s = (v_mid + spread(south[r], 1)) * jnp.where(right, x_hi, 0.02)
                a_n, l_n = face(q_n, mid[1 + r], north[r])
                a_s, l_s = face(q_s, south[r], mid[1 + r])
                a_w, l_w = faces[r]
                a_e, l_e = faces[r + 1]
                lowered = mid[1 + r] - (l_e - l_w + l_n - l_s)
                hi, lo = bounds(mid[1 + r], (mid[r], mid[2 + r], north[r], south[r]))
                gain_in, gain_out = gains(a_w, a_e, a_n, a_s)
                take_in = (right & (a_s >= 0.0)) | (jnp.logical_not(right) & (a_n < 0.0))
                gain = jnp.where(take_in, gain_in, gain_out)
                room = jnp.where(take_in, hi - lowered, lowered - lo)
                ZS[r] = ratio(gain, room)

            u = [row(0, r) for r in range(-2, 4)]
            for i, scale in enumerate((0.02, y_lo, 0.02, y_hi, 0.02)):
                CO[i] = (u[i] + u[i + 1]) * scale
            for i in range(4):
                v = row(1, i - 1)
                side = roll(mid[i], 126 - 4)
                CO[5 + i] = (v + jnp.where(last, side, roll(v, -1))) * jnp.where(last, x_hi, 0.02)
                CO[9 + i] = (v + jnp.where(first, side, roll(v, 1))) * jnp.where(first, x_lo, 0.02)

            def transport(t, extinction):
                f = t + 4
                c = [row(f, r) for r in range(-2, 4)]
                turn = 126 - 4 * f
                fe = [face(CO[i], c[i], c[i + 1]) for i in range(5)]
                lowered, ratio_in, ratio_out, an, as_ = {}, {}, {}, {}, {}
                for i in range(1, 5):
                    side = roll(ZC[i - 1], turn)
                    c_n = jnp.where(last, side, roll(c[i], -1))
                    c_s = jnp.where(first, side, roll(c[i], 1))
                    a_n, l_n = face(CO[4 + i], c[i], c_n)
                    a_s, l_s = face(CO[8 + i], c_s, c[i])
                    a_w, l_w = fe[i - 1]
                    a_e, l_e = fe[i]
                    low_c = c[i] - (l_e - l_w + l_n - l_s)
                    hi, lo = bounds(c[i], (c[i - 1], c[i + 1], c_n, c_s))
                    gain_in, gain_out = gains(a_w, a_e, a_n, a_s)
                    room_in, room_out = hi - low_c, low_c - lo
                    if i in (1, 4):
                        take_in = a_e < 0.0 if i == 1 else a_w >= 0.0
                        ratio_in[i] = ratio(
                            jnp.where(take_in, gain_in, gain_out), jnp.where(take_in, room_in, room_out)
                        )
                    else:
                        lowered[i], an[i], as_[i] = low_c, a_n, a_s
                        ratio_in[i] = ratio(gain_in, room_in)
                        ratio_out[i] = ratio(gain_out, room_out)
                a = fe[1][0]
                f_lo = a * jnp.minimum(ratio_in[1], jnp.where(a >= 0.0, ratio_in[2], ratio_out[2]))
                a = fe[2][0]
                f_mid = a * jnp.where(
                    a >= 0.0,
                    jnp.minimum(ratio_in[3], ratio_out[2]),
                    jnp.minimum(ratio_in[2], ratio_out[3]),
                )
                a = fe[3][0]
                f_hi = a * jnp.minimum(jnp.where(a >= 0.0, ratio_out[3], ratio_in[3]), ratio_in[4])
                result = []
                for i, f_w, f_e in ((2, f_lo, f_mid), (3, f_mid, f_hi)):
                    side = roll(ZS[i - 2], turn)
                    a_n, a_s = an[i], as_[i]
                    up = a_n >= 0.0
                    mine = jnp.where(up, ratio_out[i], ratio_in[i])
                    other = jnp.where(up, roll(ratio_in[i], -1), roll(ratio_out[i], -1))
                    f_n = a_n * jnp.minimum(mine, jnp.where(last, side, other))
                    at_rim = a_s * jnp.minimum(side, jnp.where(a_s >= 0.0, ratio_in[i], ratio_out[i]))
                    f_s = jnp.where(first, at_rim, roll(f_n, 1))
                    advected = lowered[i] - (f_e - f_w + f_n - f_s)
                    ADV[t, i - 2] = advected
                    result.append(extinction[i - 2] + absorb[t] * advected)
                return tuple(result)

            base_light = jnp.full((CH, 128), water_extinction, F32)
            extinction = lax.fori_loop(0, NT, transport, (base_light, base_light))

            level = k * CH + lax.broadcasted_iota(jnp.int32, (CH, 128), 0)
            wet, growth, carries = [], [], []
            for r in range(2):
                total = cumulative(extinction[r]) + carry[r]
                carries.append(carry[r] + jnp.sum(extinction[r], axis=0, keepdims=True))
                below = shortwave[pl.ds(r, 1), :] * jnp.exp(-layer_depth * total)
                sea = (land[pl.ds(r, 1), :] == 1) & (level < bottom[pl.ds(r, 1), :])
                wet.append(jnp.where(sea, 1.0, 0.0))
                grow = (
                    growth_peak
                    * jnp.exp(0.063 * row(2, r))
                    * below
                    / (below + half_light)
                    * (1.0 + 0.2 * jnp.tanh(row(3, r)))
                )
                growth.append(wet[r] * (tracer_step * grow))

            def react(o, c):
                for r in range(2):
                    mixed = reaction[o, 0] * ADV[0, r]
                    for t in range(1, NT):
                        mixed = mixed + reaction[o, t] * ADV[t, r]
                    V[s + 1, o + 4, pl.ds(base + r, CH, 2), :] = wet[r] * ADV[o, r] + growth[r] * mixed
                return c

            lax.fori_loop(0, NT, react, 0)
            return tuple(carries)

        dynamics_in = pltpu.make_async_remote_copy(
            src_ref=V.at[1, pl.ds(0, 4)],
            dst_ref=V.at[1, pl.ds(0, 4)],
            send_sem=dyn_s,
            recv_sem=dyn_r,
            device_id={"grp": 1 - grp},
            device_id_type=MESH,
        )
        dynamics_out = pltpu.make_async_copy(V.at[1, pl.ds(0, 4)], out.at[pl.ds(0, 4)], lsem.at[0])

        load.wait()
        pack(0, 0, NZ)
        pl.semaphore_wait(barrier, count + n_diag)

        def begin(k, c):
            send_rows(0, k)
            send_edges(0, k)
            return c

        lax.fori_loop(0, NK, begin, 0)

        zero = jnp.zeros((1, 128), F32)

        def first_step(k, carry):
            receive(0, k)
            carry = chunk(0, k, carry)

            @pl.when(k == 0)
            def _():
                dynamics_in.wait_recv()
                dynamics_out.start()

            send_rows(1, k)
            pack(1, k * CH, CH)
            send_edges(1, k)
            tracers_over(k).start()
            return carry

        lax.fori_loop(0, NK, first_step, (zero, zero))

        def second_step(k, carry):
            receive(1, k)
            carry = chunk(1, k, carry)
            store_out(k).start()
            return carry

        lax.fori_loop(0, NK, second_step, (zero, zero))

        def finish(k, c):
            sent(0, k)
            sent(1, k)
            tracers_over(k).wait_send()
            store_out(k).wait()
            return c

        lax.fori_loop(0, NK, finish, 0)
        dynamics_out.wait()

    def ocean_side():
        for d in range(2):
            @pl.when(jnp.logical_not(has_y[d]))
            def _():
                for s in range(STEPS):
                    fill(DH.at[s, d], 4)

            @pl.when(jnp.logical_not(has_x[d]))
            def _():
                for s in range(STEPS):
                    fill(ST.at[s, d], 2)

        lane = lanes((NZ, 128))
        four, quarter = lane % 4, lane // 4
        first_z, last_z = lane == 0, lane == 127

        def row_copy(s, d, arrival=False):
            to = d if arrival else 1 - d
            return pltpu.make_async_remote_copy(
                src_ref=D.at[s, d],
                dst_ref=DH.at[s, to],
                send_sem=ors.at[s, d],
                recv_sem=orr.at[s, to],
                device_id={"ty": ty + step_of[d]},
                device_id_type=MESH,
            )

        def col_copy(s, d, arrival=False):
            to = d if arrival else 1 - d
            return pltpu.make_async_remote_copy(
                src_ref=SS.at[s],
                dst_ref=ST.at[s, to],
                send_sem=ocs.at[s, d],
                recv_sem=ocr.at[s, to],
                device_id={"tx": tx + step_of[d]},
                device_id_type=MESH,
            )

        def exchange(s, act):
            for d in range(2):
                @pl.when(has_y[d])
                def _():
                    act(row_copy, s, d)

                @pl.when(has_x[d])
                def _():
                    act(col_copy, s, d)

        def pack(s):
            for r in range(2):
                packed = jnp.zeros((NZ, 128), F32)
                for f in range(4):
                    packed = jnp.where(quarter == f, roll(D[s, r, f], 4 * f + 2), packed)
                SS[s, r] = packed

        def light(ref):
            def body(t, acc):
                return acc + absorb[t] * ref[t + 4]

            KD[...] = lax.fori_loop(0, NT, body, jnp.full((2 * NZ, 128), water_extinction, F32))

        def update(s):
            level = lax.broadcasted_iota(jnp.int32, (NZ, 128), 0)
            for r in range(2):
                side = jnp.where(four == 1, roll(ST[s, 1, r], -1), roll(ST[s, 0, r], 1))
                own, lap, e_w, n_s = [], [], [], []
                for f in range(4):
                    c = D[s, r, f]
                    w = DH[s, 0, f] if r == 0 else D[s, 0, f]
                    e = DH[s, 1, f] if r == 1 else D[s, 1, f]
                    rim = roll(side, 126 - 4 * f)
                    n = jnp.where(last_z, rim, roll(c, -1))
                    so = jnp.where(first_z, rim, roll(c, 1))
                    own.append(c)
                    lap.append((e + w + n + so) - 4.0 * c)
                    e_w.append(e - w)
                    n_s.append(n - so)
                half = 0.5 * barotropic_gradient_coefficient
                grad_east = cumulative((-0.2 * e_w[2] + 0.8 * e_w[3]) * half)
                grad_north = cumulative((-0.2 * n_s[2] + 0.8 * n_s[3]) * half)
                extinction = KD[pl.ds(r, NZ, 2), :]
                below = shortwave[pl.ds(r, 1), :] * jnp.exp(-layer_depth * cumulative(extinction))
                above = below * jnp.exp(layer_depth * extinction)
                sea = (land[pl.ds(r, 1), :] == 1) & (level < bottom[pl.ds(r, 1), :])
                wet = jnp.where(sea, 1.0, 0.0)
                step = integration_interval
                new = (
                    own[0] + step * (coriolis * own[1] - grad_east + lap[0]),
                    own[1] + step * (-coriolis * own[0] - grad_north + lap[1]),
                    own[2] + step * (lap[2] + (above - below) / layer_depth),
                    own[3] + step * lap[3],
                )
                for f in range(4):
                    value = wet * new[f]
                    V[s + 1, f, pl.ds(r, NZ, 2), :] = value
                    if s + 1 < STEPS:
                        D[s + 1, r, f] = value

        dynamics_over = pltpu.make_async_remote_copy(
            src_ref=V.at[1, pl.ds(0, 4)],
            dst_ref=V.at[1, pl.ds(0, 4)],
            send_sem=dyn_s,
            recv_sem=dyn_r,
            device_id={"grp": 1 - grp},
            device_id_type=MESH,
        )

        def tracers_in(k):
            rows = pl.ds(pl.multiple_of(k * 16, 16), 16)
            return pltpu.make_async_remote_copy(
                src_ref=V.at[1, pl.ds(4, NT), rows],
                dst_ref=V.at[2, pl.ds(4, NT), rows],
                send_sem=tra_s.at[k],
                recv_sem=tra_r.at[k],
                device_id={"grp": 1 - grp},
                device_id_type=MESH,
            )

        load.wait()
        for r in range(2):
            for f in range(4):
                D[0, r, f] = V[0, f, pl.ds(r, NZ, 2), :]
        pack(0)
        pl.semaphore_wait(barrier, count)
        exchange(0, lambda copy, s, d: copy(s, d).start())
        light(V.at[0])
        exchange(0, lambda copy, s, d: copy(s, d, True).wait_recv())
        update(0)
        dynamics_over.start()
        pack(1)
        exchange(1, lambda copy, s, d: copy(s, d).start())

        def tracers_out(k):
            rows = pl.ds(pl.multiple_of(k * 16, 16), 16)
            return pltpu.make_async_copy(V.at[2, pl.ds(4, NT), rows], out.at[pl.ds(4, NT), rows], lsem.at[1 + k])

        def arrive(k, c):
            tracers_in(k).wait_recv()
            tracers_out(k).start()
            return c

        lax.fori_loop(0, NK, arrive, 0)
        light(V.at[2])
        exchange(1, lambda copy, s, d: copy(s, d, True).wait_recv())
        update(1)
        dynamics_out = pltpu.make_async_copy(V.at[2, pl.ds(0, 4)], out.at[pl.ds(0, 4)], lsem.at[0])
        dynamics_out.start()
        exchange(0, lambda copy, s, d: copy(s, d).wait_send())
        exchange(1, lambda copy, s, d: copy(s, d).wait_send())
        dynamics_over.wait_send()

        def finish(k, c):
            tracers_out(k).wait()
            return c

        lax.fori_loop(0, NK, finish, 0)
        dynamics_out.wait()

    pl.when(grp == 1)(tracer_side)
    pl.when(grp == 0)(ocean_side)


def local(coupled_state, land_mask, bottom_level, shortwave, absorb, reaction):
    x = coupled_state.reshape(NF, 2 * NZ, 128)
    vmem, smem, anywhere = (
        pl.BlockSpec(memory_space=pltpu.VMEM),
        pl.BlockSpec(memory_space=pltpu.SMEM),
        pl.BlockSpec(memory_space=pl.ANY),
    )
    dma = pltpu.SemaphoreType.DMA
    y = pl.pallas_call(
        kernel,
        out_shape=jax.ShapeDtypeStruct((NF, 2 * NZ, 128), F32),
        in_specs=[anywhere, vmem, vmem, vmem, smem, smem],
        out_specs=anywhere,
        scratch_shapes=[
            pltpu.VMEM((STEPS + 1, NF, 2 * NZ, 128), F32),
            pltpu.VMEM((STEPS, 2, NF, 2 * NZ, 128), F32),
            pltpu.VMEM((STEPS, 2, NZ, 128), F32),
            pltpu.VMEM((STEPS, 2, 2, NZ, 128), F32),
            pltpu.VMEM((STEPS, 4, NZ, 128), F32),
            pltpu.VMEM((NT, 2, CH, 128), F32),
            pltpu.VMEM((13, CH, 128), F32),
            pltpu.VMEM((4, CH, 128), F32),
            pltpu.VMEM((2, CH, 128), F32),
            pltpu.VMEM((STEPS, 2, 4, NZ, 128), F32),
            pltpu.VMEM((STEPS, 2, 4, NZ, 128), F32),
            pltpu.VMEM((STEPS, 2, NZ, 128), F32),
            pltpu.VMEM((STEPS, 2, 2, NZ, 128), F32),
            pltpu.VMEM((2 * NZ, 128), F32),
            dma((1 + NK,)),
            dma((STEPS, 2, NK, 2)),
            dma((STEPS, 2, NK, 2)),
            dma((STEPS, 2, NK)),
            dma((STEPS, 2, NK)),
            dma((STEPS, 4, NK)),
            dma((STEPS, 4, NK)),
            dma,
            dma,
            dma((NK,)),
            dma((NK,)),
            dma((STEPS, 2)),
            dma((STEPS, 2)),
            dma((STEPS, 2)),
            dma((STEPS, 2)),
        ],
        compiler_params=pltpu.CompilerParams(
            collective_id=0, has_side_effects=True, vmem_limit_bytes=32 * 1024 * 1024
        ),
    )(x, land_mask, bottom_level, shortwave, absorb, reaction)
    return y.reshape(1, NF, NZ, 2, 128)


def solution(mesh):
    in_specs = (
        P("grp", None, None, "ty", "tx"),
        P("ty", "tx"),
        P("ty", "tx"),
        P("ty", "tx"),
        P(),
        P(),
    )
    out_specs = P("grp", None, None, "ty", "tx")
    return jax.shard_map(local, mesh=mesh, in_specs=in_specs, out_specs=out_specs, check_vma=False)
```

profile of v0, /device:TPU:7, one launch (start us, length us, event | category | flops | bytes accessed | tf_op | source)
XLA Modules:
  0.0 71.6 jit_solution(3330319996156872075)
XLA Ops:
  0.0 0.0 copy-start.5
  0.0 0.0 copy-start.2
  0.0 0.7 copy-done.5
  0.7 0.0 copy-done.2
  0.7 0.0 copy-start
  0.7 1.1 %copy-done = f32[1,23,32,2,128]{4,3,2,1,0:T(2,128)S(1)} copy-done((f32[1,23,32,2,128]{4,3,2,1,0:T(2,128)S(1)}, f32[1,23,32,2,128]{4,3,2,1,0:T(2,128)}, u32[]{:S(2)}) %copy-start) | copy-done | bytes 753688
  1.8 0.0 copy-start.1
  1.8 0.7 copy-done.1
  2.5 0.0 copy-start.3
  2.5 0.7 copy-done.3
  3.2 0.0 copy-start.4
  3.2 0.7 copy-done.4
  3.9 66.9 %shard_map.64 = f32[23,64,128]{2,1,0:T(8,128)S(1)} custom-call(f32[23,64,128]{2,1,0:T(8,128)S(1)} %bitcast.3, s32[2,128]{1,0:T(2,128)S(1)} %copy-done.2, s32[2,128]{1,0:T(2,128)S(1)} %copy-done.3, f32[2,128]{1,0:T(2,128)S(1)} %copy-done.4, f32[19]{0:T(128)S(1)} %copy-done.5, f32[19,19]{1,0:T(8,128)S(1)} %copy-done.1), custom_call_target="tpu_custom_call" | custom-call | tf_op jit(solution)/shard_map/pallas_call | solution.py:644
  70.7 0.9 %copy.8 = f32[1,23,32,2,128]{4,3,2,1,0:T(2,128)} copy(f32[1,23,32,2,128]{4,3,2,1,0:T(2,128)S(1)} %bitcast.2) | data formatting | bytes 1507328
Async XLA Ops:
  0.0 0.7 copy-start.5
  0.0 0.7 copy-start.2
  0.7 1.1 %copy-start = (f32[1,23,32,2,128]{4,3,2,1,0:T(2,128)S(1)}, f32[1,23,32,2,128]{4,3,2,1,0:T(2,128)}, u32[]{:S(2)}) copy-start(f32[1,23,32,2,128]{4,3,2,1,0:T(2,128)} %param.6) | copy-start | bytes 2260996
  1.8 0.7 copy-start.1
  2.5 0.7 copy-start.3
  3.2 0.7 copy-start.4
where the time goes:
time: 71.9 us; the launch traced here: 71.6 us
  Pallas kernels  66.9 us (93%)
  local copies, waits for them, and re-layouts  4.75 us (7%)
    pallas_call x1, Pallas kernels, local(): pl.pallas_call(kernel, out_shape=jax.ShapeDtypeStruct((NF, 2 * NZ, 128),...  66.9 us
    unnamed x13, local copies, waits for them, and re-layouts  4.75 us

commit v1 on v0

--- a/solution.py
+++ b/solution.py
@@ -53,9 +53,9 @@
 
 
 def kernel(
-    x, land, bottom, shortwave, absorb, reaction, out,
-    V, H, PS, PT, PD, ADV, CO, ZC, ZS, D, DH, SS, ST, KD,
-    lsem, row_s, row_r, col_s, col_r, diag_s, diag_r, dyn_s, dyn_r, tra_s, tra_r, ors, orr, ocs, ocr,
+    x, land_in, bottom_in, shortwave_in, absorb_in, reaction_in, out,
+    V, H, PS, PT, PD, ADV, CO, ZC, ZS, D, DH, SS, ST, KD, land, bottom, shortwave, absorb, reaction,
+    lsem, psem, row_s, row_r, col_s, col_r, diag_s, diag_r, dyn_s, dyn_r, tra_s, tra_r, ors, orr, ocs, ocr,
 ):
     grp, ty, tx = lax.axis_index("grp"), lax.axis_index("ty"), lax.axis_index("tx")
     nty, ntx = lax.axis_size("ty"), lax.axis_size("tx")
@@ -83,6 +83,20 @@
 
     load = pltpu.make_async_copy(x, V.at[0], lsem.at[0])
     load.start()
+    small = [
+        pltpu.make_async_copy(source, to, psem.at[i])
+        for i, (source, to) in enumerate(
+            (
+                (land_in, land),
+                (bottom_in, bottom),
+                (shortwave_in, shortwave),
+                (absorb_in, absorb),
+                (reaction_in, reaction),
+            )
+        )
+    ]
+    for copy in small:
+        copy.start()
 
     def fill(ref, n):
         def body(i, c):
@@ -240,7 +254,7 @@
                 )
 
             zero = jnp.zeros((count, 128), F32)
-            packed = lax.fori_loop(0, NF, body, (zero, zero))
+            packed = lax.fori_loop(0, NF, body, (zero, zero), unroll=True)
             for r in range(2):
                 PS[s, r, pl.ds(start, count), :] = packed[r]
 
@@ -383,7 +397,7 @@
                 return tuple(result)
 
             base_light = jnp.full((CH, 128), water_extinction, F32)
-            extinction = lax.fori_loop(0, NT, transport, (base_light, base_light))
+            extinction = lax.fori_loop(0, NT, transport, (base_light, base_light), unroll=True)
 
             level = k * CH + lax.broadcasted_iota(jnp.int32, (CH, 128), 0)
             wet, growth, carries = [], [], []
@@ -410,7 +424,7 @@
                     V[s + 1, o + 4, pl.ds(base + r, CH, 2), :] = wet[r] * ADV[o, r] + growth[r] * mixed
                 return c
 
-            lax.fori_loop(0, NT, react, 0)
+            lax.fori_loop(0, NT, react, 0, unroll=True)
             return tuple(carries)
 
         dynamics_in = pltpu.make_async_remote_copy(
@@ -424,6 +438,8 @@
         dynamics_out = pltpu.make_async_copy(V.at[1, pl.ds(0, 4)], out.at[pl.ds(0, 4)], lsem.at[0])
 
         load.wait()
+        for copy in small:
+            copy.wait()
         pack(0, 0, NZ)
         pl.semaphore_wait(barrier, count + n_diag)
 
@@ -590,6 +606,8 @@
             )
 
         load.wait()
+        for copy in small:
+            copy.wait()
         for r in range(2):
             for f in range(4):
                 D[0, r, f] = V[0, f, pl.ds(r, NZ, 2), :]
@@ -635,17 +653,13 @@
 
 def local(coupled_state, land_mask, bottom_level, shortwave, absorb, reaction):
     x = coupled_state.reshape(NF, 2 * NZ, 128)
-    vmem, smem, anywhere = (
-        pl.BlockSpec(memory_space=pltpu.VMEM),
-        pl.BlockSpec(memory_space=pltpu.SMEM),
-        pl.BlockSpec(memory_space=pl.ANY),
-    )
+    hbm = pl.BlockSpec(memory_space=pltpu.HBM)
     dma = pltpu.SemaphoreType.DMA
     y = pl.pallas_call(
         kernel,
         out_shape=jax.ShapeDtypeStruct((NF, 2 * NZ, 128), F32),
-        in_specs=[anywhere, vmem, vmem, vmem, smem, smem],
-        out_specs=anywhere,
+        in_specs=[hbm] * 6,
+        out_specs=hbm,
         scratch_shapes=[
             pltpu.VMEM((STEPS + 1, NF, 2 * NZ, 128), F32),
             pltpu.VMEM((STEPS, 2, NF, 2 * NZ, 128), F32),
@@ -661,7 +675,13 @@
             pltpu.VMEM((STEPS, 2, NZ, 128), F32),
             pltpu.VMEM((STEPS, 2, 2, NZ, 128), F32),
             pltpu.VMEM((2 * NZ, 128), F32),
+            pltpu.VMEM((2, 128), jnp.int32),
+            pltpu.VMEM((2, 128), jnp.int32),
+            pltpu.VMEM((2, 128), F32),
+            pltpu.SMEM((NT,), F32),
+            pltpu.SMEM((NT, NT), F32),
             dma((1 + NK,)),
+            dma((5,)),
             dma((STEPS, 2, NK, 2)),
             dma((STEPS, 2, NK, 2)),
             dma((STEPS, 2, NK)),
@@ -678,7 +698,7 @@
             dma((STEPS, 2)),
         ],
         compiler_params=pltpu.CompilerParams(
-            collective_id=0, has_side_effects=True, vmem_limit_bytes=32 * 1024 * 1024
+            collective_id=0, has_side_effects=True
         ),
     )(x, land_mask, bottom_level, shortwave, absorb, reaction)
     return y.reshape(1, NF, NZ, 2, 128)

time: 71.9 us -> 33 us (0.46)
  Pallas kernels: 66.9 us -> 30.7 us
  local copies, waits for them, and re-layouts: 4.75 us -> 2.07 us
    pallas_call x1, Pallas kernels: 66.9 us -> 30.7 us  [local(): pl.pallas_call(kernel, out_shape=jax.ShapeDtypeStruct((NF, 2 * NZ, 128),...]
    unnamed x13 -> x1, local copies, waits for them, and re-layouts: 4.75 us -> 2.07 us
where the time goes in v1:
time: 33 us; the launch traced here: 32.8 us
  Pallas kernels  30.7 us (93%)
  local copies, waits for them, and re-layouts  2.07 us (6%)
    pallas_call x1, Pallas kernels, local(): pl.pallas_call(kernel, out_shape=jax.ShapeDtypeStruct((NF, 2 * NZ, 128),...  30.7 us
    unnamed x1, local copies, waits for them, and re-layouts  2.07 us

profile of v1, /device:TPU:7, one launch (start us, length us, event | category | flops | bytes accessed | tf_op | source)
XLA Modules:
  0.0 32.8 jit_solution(14862300878643215722)
XLA Ops:
  0.0 30.7 %shard_map.64 = f32[23,64,128]{2,1,0:T(8,128)} custom-call(f32[23,64,128]{2,1,0:T(8,128)} %bitcast.3, s32[2,128]{1,0:T(2,128)} %land_in.1, s32[2,128]{1,0:T(2,128)} %bottom_in.1, f32[2,128]{1,0:T(2,128)} %shortwave_in.1, f32[19]{0:T(128)} %absorb_in.1, f32[19,19]{1,0:T(8,128)} %reaction_in.1), custom_call_target="tpu_custom_call" | custom-call | tf_op jit(solution)/shard_map/pallas_call | solution.py:658
  30.7 2.1 %copy.8 = f32[1,23,32,2,128]{4,3,2,1,0:T(2,128)} copy(f32[1,23,32,2,128]{4,3,2,1,0:T(2,128)} %bitcast.2) | data formatting | bytes 1507328

commit v2 on v1

--- a/solution.py
+++ b/solution.py
@@ -444,11 +444,11 @@
         pl.semaphore_wait(barrier, count + n_diag)
 
         def begin(k, c):
-            send_rows(0, k)
             send_edges(0, k)
             return c
 
         lax.fori_loop(0, NK, begin, 0)
+        lax.fori_loop(0, NK, lambda k, c: (send_rows(0, k), c)[1], 0)
 
         zero = jnp.zeros((1, 128), F32)
 
@@ -461,9 +461,9 @@
                 dynamics_in.wait_recv()
                 dynamics_out.start()
 
-            send_rows(1, k)
             pack(1, k * CH, CH)
             send_edges(1, k)
+            send_rows(1, k)
             tracers_over(k).start()
             return carry
 

time: 33 us -> 32.5 us (0.985)
  Pallas kernels: 30.7 us -> 30.2 us
    pallas_call x1, Pallas kernels: 30.7 us -> 30.2 us  [local(): pl.pallas_call(kernel, out_shape=jax.ShapeDtypeStruct((NF, 2 * NZ, 128),...]
where the time goes in v2:
time: 32.5 us; the launch traced here: 32.3 us
  Pallas kernels  30.2 us (93%)
  local copies, waits for them, and re-layouts  2.07 us (6%)
    pallas_call x1, Pallas kernels, local(): pl.pallas_call(kernel, out_shape=jax.ShapeDtypeStruct((NF, 2 * NZ, 128),...  30.2 us
    unnamed x1, local copies, waits for them, and re-layouts  2.07 us

profile of v2, /device:TPU:7, one launch (start us, length us, event | category | flops | bytes accessed | tf_op | source)
XLA Modules:
  0.0 32.3 jit_solution(7330165840653330049)
XLA Ops:
  0.0 30.2 %shard_map.64 = f32[23,64,128]{2,1,0:T(8,128)} custom-call(f32[23,64,128]{2,1,0:T(8,128)} %bitcast.3, s32[2,128]{1,0:T(2,128)} %land_in.1, s32[2,128]{1,0:T(2,128)} %bottom_in.1, f32[2,128]{1,0:T(2,128)} %shortwave_in.1, f32[19]{0:T(128)} %absorb_in.1, f32[19,19]{1,0:T(8,128)} %reaction_in.1), custom_call_target="tpu_custom_call" | custom-call | tf_op jit(solution)/shard_map/pallas_call | solution.py:658
  30.2 2.1 %copy.8 = f32[1,23,32,2,128]{4,3,2,1,0:T(2,128)} copy(f32[1,23,32,2,128]{4,3,2,1,0:T(2,128)} %bitcast.2) | data formatting | bytes 1507328

commit v3 on v2

--- a/solution.py
+++ b/solution.py
@@ -137,7 +137,7 @@
 
         def row_copy(s, d, k, part):
             lo, n = ((0, 2), (4, NT))[part]
-            rows = pl.ds(pl.multiple_of(k * 16, 16), 16)
+            rows = pl.ds(pl.multiple_of(k * 16, 16), 16) if part else pl.ds(0, 2 * NZ)
             src = (x if s == 0 else V.at[s]).at[pl.ds(lo, n), rows]
             return pltpu.make_async_remote_copy(
                 src_ref=src,
@@ -150,7 +150,7 @@
 
         def row_arrival(s, d, k, part):
             lo, n = ((0, 2), (4, NT))[part]
-            rows = pl.ds(pl.multiple_of(k * 16, 16), 16)
+            rows = pl.ds(pl.multiple_of(k * 16, 16), 16) if part else pl.ds(0, 2 * NZ)
             return pltpu.make_async_remote_copy(
                 src_ref=V.at[s, pl.ds(lo, n), rows],
                 dst_ref=H.at[s, d, pl.ds(lo, n), rows],
@@ -185,12 +185,27 @@
                 device_id_type=MESH,
             )
 
+        def tracer_rows(s, k, act):
+            for d in range(2):
+                @pl.when(has_y[d])
+                def _():
+                    act(s, d, k, 1)
+
+        def velocity_rows(s, act):
+            for d in range(2):
+                @pl.when(has_y[d])
+                def _():
+                    act(s, d, 0, 0)
+
         def each_row(s, k, act):
             for d in range(2):
+                @pl.when(has_y[d] & (k == 0))
+                def _():
+                    act(s, d, 0, 0)
+
                 @pl.when(has_y[d])
                 def _():
-                    for part in range(2):
-                        act(s, d, k, part)
+                    act(s, d, k, 1)
 
         def send_rows(s, k):
             each_row(s, k, lambda *a: row_copy(*a).start())
@@ -458,12 +473,18 @@
 
             @pl.when(k == 0)
             def _():
+                tracer_rows(1, k, lambda *a: row_copy(*a).start())
                 dynamics_in.wait_recv()
                 dynamics_out.start()
+                velocity_rows(1, lambda *a: row_copy(*a).start())
 
             pack(1, k * CH, CH)
             send_edges(1, k)
-            send_rows(1, k)
+
+            @pl.when(k > 0)
+            def _():
+                tracer_rows(1, k, lambda *a: row_copy(*a).start())
+
             tracers_over(k).start()
             return carry
 

time: 32.5 us -> 32.5 us (level)
  no operation moved by 1% of the time
where the time goes in v3:
time: 32.5 us; the launch traced here: 32.3 us
  Pallas kernels  30.2 us (93%)
  local copies, waits for them, and re-layouts  2.07 us (6%)
    pallas_call x1, Pallas kernels, local(): pl.pallas_call(kernel, out_shape=jax.ShapeDtypeStruct((NF, 2 * NZ, 128),...  30.2 us
    unnamed x1, local copies, waits for them, and re-layouts  2.07 us

profile of v3, /device:TPU:7, one launch (start us, length us, event | category | flops | bytes accessed | tf_op | source)
XLA Modules:
  0.0 32.3 jit_solution(2397999513262778188)
XLA Ops:
  0.0 30.2 %shard_map.64 = f32[23,64,128]{2,1,0:T(8,128)} custom-call(f32[23,64,128]{2,1,0:T(8,128)} %bitcast.3, s32[2,128]{1,0:T(2,128)} %land_in.1, s32[2,128]{1,0:T(2,128)} %bottom_in.1, f32[2,128]{1,0:T(2,128)} %shortwave_in.1, f32[19]{0:T(128)} %absorb_in.1, f32[19,19]{1,0:T(8,128)} %reaction_in.1), custom_call_target="tpu_custom_call" | custom-call | tf_op jit(solution)/shard_map/pallas_call | solution.py:679
  30.2 2.1 %copy.8 = f32[1,23,32,2,128]{4,3,2,1,0:T(2,128)} copy(f32[1,23,32,2,128]{4,3,2,1,0:T(2,128)} %bitcast.2) | data formatting | bytes 1507328
